TPU v7x, 256 devices: a whole 4x4x8 slice. The times are simulated.
256 devices in a mesh: inp: 8 (over z_hi, x), out: 4 (over z_lo), dep: 8 (over y, core).
Axes of the slice: x: 4, y: 4, z: 8 (z_hi: 2, z_lo: 4; z = z_hi * 4 + z_lo), core: 2. Of those that a mesh axis runs over, the one named last changes fastest.
Arguments:
- tokens: bfloat16 [4096, 6144], P(('dep', 'out'), 'inp'), may hold values from -6 to 6
- up_weight: bfloat16 [6144, 24576], P(('inp', 'dep'), 'out'), may hold values from -0.078125 to 0.078125
- hidden_grad: bfloat16 [4096, 24576], P(('dep', 'inp'), 'out'), may hold values from -6 to 6
Outputs:
- hidden: bfloat16 [4096, 24576], P(('dep', 'inp'), 'out')
- input_grad: bfloat16 [4096, 6144], P(('dep', 'out'), 'inp')
- weight_grad: float32 [6144, 24576], P(('inp', 'dep'), 'out')
All inputs are finite; a program needn't handle non-finite values.
Results may differ from a plain program's by a relative error of at most 0.022.
Values may be sent and summed in bfloat16 or wider, within the bound.
A program may use at most 128 MiB of HBM per device.

v0:
```python
import math

import jax
import jax.numpy as jnp
from jax import lax
from jax.sharding import PartitionSpec as P


def activation(values):
    return jax.nn.gelu(values, approximate=True)


def on_device(tokens, up_weight, hidden_grad):
    gathered_x = lax.all_gather(tokens, "out", axis=0, tiled=True)
    group_rows = gathered_x.shape[0]
    full_weight = lax.all_gather(up_weight, "dep", axis=0, tiled=True)
    block = gathered_x
    pre = lax.psum_scatter(
        jnp.dot(block, full_weight, preferred_element_type=jnp.float32).astype(jnp.bfloat16),
        "inp",
        scatter_dimension=0,
        tiled=True,
    ).astype(jnp.float32)
    hidden = activation(pre).astype(jnp.bfloat16)
    _, pullback = jax.vjp(activation, pre)
    grad_pre = pullback(hidden_grad.astype(jnp.float32))[0].astype(jnp.bfloat16)
    gathered_grad = lax.all_gather(grad_pre, "inp", axis=0, tiled=True)
    block = gathered_grad
    input_sum = lax.psum_scatter(
        lax.dot_general(
            block, full_weight, (((1,), (1,)), ((), ())), preferred_element_type=jnp.float32
        ).astype(jnp.bfloat16),
        "out",
        scatter_dimension=0,
        tiled=True,
    )
    weight_total = lax.psum_scatter(
        lax.dot_general(
            gathered_x, gathered_grad, (((0,), (0,)), ((), ())), preferred_element_type=jnp.float32
        ).astype(jnp.bfloat16),
        "dep",
        scatter_dimension=0,
        tiled=True,
    ).astype(jnp.float32)
    all_tokens = group_rows * lax.axis_size("dep")
    weight_grad = weight_total * (1.0 / math.sqrt(all_tokens))
    return (hidden, input_sum, weight_grad)


def solution(mesh):
    placed = (P(("dep", "out"), "inp"), P(("inp", "dep"), "out"), P(("dep", "inp"), "out"))
    return jax.shard_map(
        on_device,
        mesh=mesh,
        in_specs=placed,
        out_specs=(P(("dep", "inp"), "out"), P(("dep", "out"), "inp"), P(("inp", "dep"), "out")),
        check_vma=False,
    )
```

profile of v0, /device:TPU:2, one launch (start us, length us, event | category | flops | bytes accessed | tf_op | source)
XLA Modules:
  0.0 489.9 jit_solution(702694919154467806)
XLA Ops:
  7.2 0.0 all-gather.3.cloned.1.call-start
  7.2 0.7 all-gather.3.cloned.1.call-update
  7.9 0.0 reduce-scatter.6.cloned.1.call-start
  7.9 21.1 %all_gather.9 = bf16[512,768]{1,0:T(8,128)(2,1)S(1)} all-gather(bf16[128,768]{1,0:T(8,128)(2,1)} %param.3), channel_id=1, replica_groups=mesh['inp'=8,'out'=4,'dep'=8] {'out'}, dimensions={0}, use_global_device_ids=true | all-gather | bytes 983040 | tf_op jit(solution)/shard_map/all_gather | solution.py:14
  29.0 40.5 %all-gather.3.cloned.1.call-done = bf16[768,6144]{1,0:T(8,128)(2,1)} async-done(((bf16[96,6144]{1,0:T(8,128)(2,1)}), bf16[768,6144]{1,0:T(8,128)(2,1)}) %all-gather.3.cloned.1.call-update) | async-done | bytes 9437200 | tf_op jit(solution)/shard_map/all_gather | solution.py:16
  69.5 10.6 %convolution_convert_fusion.1 = bf16[512,6144]{1,0:T(8,128)(2,1)} fusion(bf16[512,768]{1,0:T(8,128)(2,1)S(1)} %all_gather.9, bf16[768,6144]{1,0:T(8,128)(2,1)} %all-gather.3.cloned.1.call-done), kind=kOutput, calls=%fused_computation.2 | convolution fusion | flops 4834983936 | bytes 16515072 | tf_op jit(solution)/shard_map/dot_general | solution.py:19
  80.1 0.0 copy-start
  80.1 0.0 reduce-scatter.6.cloned.1.call-update
  80.1 0.0 all-gather.5.cloned.1.call-start
  80.1 154.3 %reduce-scatter.6.cloned.1.call-done = bf16[64,6144]{1,0:T(8,128)(2,1)} async-done(((bf16[512,6144]{1,0:T(8,128)(2,1)}), bf16[64,6144]{1,0:T(8,128)(2,1)}) %reduce-scatter.6.cloned.1.call-update) | async-done | bytes 786448 | tf_op jit(solution)/shard_map/reduce_scatter | solution.py:18
  234.4 0.0 copy-done
  234.4 3.5 fusion.4
  237.9 0.0 all-gather.5.cloned.1.call-update
  238.0 0.0 reduce-scatter.10.cloned.1.call-start
  238.0 135.0 %all-gather.5.cloned.1.call-done = bf16[512,6144]{1,0:T(8,128)(2,1)} async-done(((bf16[64,6144]{1,0:T(8,128)(2,1)}), bf16[512,6144]{1,0:T(8,128)(2,1)}) %all-gather.5.cloned.1.call-update) | async-done | bytes 6291472 | tf_op jit(solution)/shard_map/all_gather | solution.py:27
  373.0 10.3 %fusion = bf16[768,6144]{0,1:T(8,128)(2,1)} fusion(bf16[512,6144]{1,0:T(8,128)(2,1)} %all-gather.5.cloned.1.call-done, bf16[512,768]{1,0:T(8,128)(2,1)S(1)} %all_gather.9), kind=kOutput, calls=%fused_computation.1 | convolution fusion | flops 4836556800 | bytes 16515072 | tf_op jit(solution)/shard_map/dot_general | solution.py:38
  383.3 12.7 %copy.8 = bf16[768,6144]{1,0:T(8,128)(2,1)} copy(bf16[768,6144]{0,1:T(8,128)(2,1)} %fusion) | data formatting | bytes 18874368
  396.0 0.0 reduce-scatter.10.cloned.1.call-update
  396.0 0.0 reduce-scatter.8.cloned.1.call-start
  396.1 10.7 %convolution_convert_fusion.2 = bf16[512,768]{1,0:T(8,128)(2,1)} fusion(bf16[512,6144]{1,0:T(8,128)(2,1)} %all-gather.5.cloned.1.call-done, bf16[768,6144]{1,0:T(8,128)(2,1)} %all-gather.3.cloned.1.call-done), kind=kOutput, calls=%fused_computation.21 | convolution fusion | flops 4832231424 | bytes 16515072 | tf_op jit(solution)/shard_map/dot_general | solution.py:30
  406.8 0.0 reduce-scatter.8.cloned.1.call-update
  406.8 45.2 %reduce-scatter.10.cloned.1.call-done = bf16[96,6144]{1,0:T(8,128)(2,1)} async-done(((bf16[768,6144]{1,0:T(8,128)(2,1)}), bf16[96,6144]{1,0:T(8,128)(2,1)}) %reduce-scatter.10.cloned.1.call-update) | async-done | bytes 1179664
  452.0 2.5 copy.9
  454.5 1.6 convert_multiply_fusion
  456.1 2.2 copy.7
  458.3 25.1 %reduce-scatter.8.cloned.1.call-done = bf16[128,768]{1,0:T(8,128)(2,1)} async-done(((bf16[512,768]{1,0:T(8,128)(2,1)}), bf16[128,768]{1,0:T(8,128)(2,1)}) %reduce-scatter.8.cloned.1.call-update) | async-done | bytes 196624 | tf_op jit(solution)/shard_map/reduce_scatter | solution.py:29
Async XLA Ops:
  7.2 62.3 %all-gather.3.cloned.1.call-start = ((), (), s32[]{:S(2)}) async-start(), calls=%async_computation.3 | async-start | bytes 10616832 | tf_op jit(solution)/shard_map/all_gather | solution.py:16
  7.9 226.5 %reduce-scatter.6.cloned.1.call-start = ((), (), s32[]{:S(2)}) async-start(), calls=%async_computation.4 | async-start | bytes 7077888 | tf_op jit(solution)/shard_map/reduce_scatter | solution.py:18
  80.1 154.4 %copy-start = (bf16[64,6144]{1,0:T(8,128)(2,1)S(1)}, bf16[64,6144]{1,0:T(8,128)(2,1)}, u32[]{:S(2)}) copy-start(bf16[64,6144]{1,0:T(8,128)(2,1)} %param.5) | copy-start | bytes 2359300
  80.1 292.9 %all-gather.5.cloned.1.call-start = ((), (), s32[]{:S(2)}) async-start(), calls=%async_computation.5 | async-start | bytes 7077888 | tf_op jit(solution)/shard_map/all_gather | solution.py:27
  238.0 214.0 %reduce-scatter.10.cloned.1.call-start = ((), (), s32[]{:S(2)}) async-start(), calls=%async_computation.7 | async-start | bytes 10616832
  396.0 87.3 %reduce-scatter.8.cloned.1.call-start = ((), (), s32[]{:S(2)}) async-start(), calls=%async_computation.6 | async-start | bytes 983040 | tf_op jit(solution)/shard_map/reduce_scatter | solution.py:29
Sparse Core Ops, SparseCore 0:
  9.8 59.6 all-gather.2
  80.2 154.1 reduce-scatter.5
  238.1 134.9 all-gather.4
  396.1 55.7 reduce-scatter.9
  455.1 28.1 reduce-scatter.7
where the time goes:
time: 490 us
  waiting for transfers between devices  401 us (82%)
  matrix products  31.6 us (6%)
  blocking collectives  21.1 us (4%)
  local copies, waits for them, and re-layouts  17.4 us (4%)
  between operations  13.8 us (3%)
  other arithmetic  5.11 us (1%)
    reduce_scatter x1, waiting for transfers between devices, on_device(): lax.psum_scatter(jnp.dot(block, full_weight, preferred_element_type=jnp.f...  154 us
    all_gather x1, waiting for transfers between devices, on_device(): gathered_grad = lax.all_gather(grad_pre, 'inp', axis=0, tiled=True)  135 us
    unnamed x6, waiting for transfers between devices  45.9 us
    all_gather x1, waiting for transfers between devices, on_device(): full_weight = lax.all_gather(up_weight, 'dep', axis=0, tiled=True)  40.5 us
    reduce_scatter x1, waiting for transfers between devices, on_device(): lax.psum_scatter(lax.dot_general(block, full_weight, (((1,), (1,)), ((),...  25.1 us
    all_gather x1, blocking collectives, on_device(): gathered_x = lax.all_gather(tokens, 'out', axis=0, tiled=True)  21.1 us
    unnamed x5, local copies, waits for them, and re-layouts  17.4 us
    dot_general x1, matrix products, on_device(): lax.dot_general(block, full_weight, (((1,), (1,)), ((), ())), preferred_e...  10.7 us
  transfers between devices with their start and end apart: 5, of which 5 were waited for; matrix products, arithmetic and copies ran while one was open for 3% of the time, Pallas kernels for 0%

commit v1 on v0

v1 whole, which is shorter than its diff:
```python
import functools
import math

import jax
import jax.numpy as jnp
from jax import lax
from jax.experimental import pallas as pl
from jax.experimental.pallas import tpu as pltpu
from jax.sharding import PartitionSpec as P

MESH = pl.DeviceIdType.MESH
BF, F32 = jnp.bfloat16, jnp.float32

NX, NY, NL = 4, 4, 4
C, NC = 256, 12
HALF = C * NC
SUB = 64
ROWS = 96
D = 768

FLOWS = (
    "w_core", "w_up", "w_down", "w_up2", "w_down2", "hg_core",
    "s1_up", "s1_down", "s2_up", "s2_down", "z_pre", "z_grad",
    "g_up", "g_down", "g_up2", "g_down2", "hid_core",
    "q1_up", "q1_down", "q2_up", "q2_down", "wg_core",
)


def act_and_slope(v):
    a, b = math.sqrt(2.0 / math.pi), 0.044715
    sq = v * v
    t = jnp.tanh(a * v * (1.0 + b * sq))
    half = 0.5 * (1.0 + t)
    return v * half, half + (0.5 * a) * v * (1.0 - t * t) * (1.0 + (3.0 * b) * sq)


def kernel(
    tok_in, w_in, hg_in, hid_out, ig_out, wg_out,
    tok, tok_t, wbuf, hgb, part, r1, r2, zs, r3, tot, grad, hs, q, r8, r9, ws, acc, cs, cr,
    lr_send, lr_recv, ll_send, ll_recv, ig_buf,
    f_send, f_recv, w_loc, hg_loc, hid_loc, wg_loc, one_loc,
    t_recv, tc_recv, t_send, tc_send, c_sem, lr_sems, ll_sems,
):
    inp, l, dep = lax.axis_index("inp"), lax.axis_index("out"), lax.axis_index("dep")
    h, x = inp // NX, inp % NX
    y, c = dep // 2, dep % 2
    o = 1 - c

    def dev(h_=h, x_=x, l_=l, y_=y, c_=c):
        return (h_ * NX + x_, l_, y_ * 2 + c_)

    x_up, x_dn, x_far = (x + 1) % NX, (x + 3) % NX, (x + 2) % NX
    y_up, y_dn, y_far = (y + 1) % NY, (y + 3) % NY, (y + 2) % NY
    d_xu, d_xd, d_yu, d_yd = dev(x_=x_up), dev(x_=x_dn), dev(y_=y_up), dev(y_=y_dn)
    d_c, d_z = dev(c_=o), dev(h_=1 - h)
    zpos = h * NL + l
    zu, zd = (zpos + 1) % (2 * NL), (zpos + 2 * NL - 1) % (2 * NL)
    d_zu, d_zd = dev(h_=zu // NL, l_=zu % NL), dev(h_=zd // NL, l_=zd % NL)

    def rc(src, dst, ss, rs, to):
        return pltpu.make_async_remote_copy(
            src_ref=src, dst_ref=dst, send_sem=ss, recv_sem=rs, device_id=to, device_id_type=MESH
        )

    def cols(k, which):
        return pl.ds(pl.multiple_of(which * HALF + k * C, C), C)

    def w_rows(who):
        return pl.ds(pl.multiple_of(who * ROWS, 16), ROWS)

    top, bottom = pl.ds(0, ROWS), pl.ds(ROWS, ROWS)
    table = {
        "w_core": (lambda k: w_in.at[:, cols(k, o)], lambda k: wbuf.at[k, y, w_rows(c)],
                   d_c, lambda k: wbuf.at[k, y, w_rows(o)]),
        "w_up": (lambda k: wbuf.at[k, y], lambda k: wbuf.at[k, y], d_yu, lambda k: wbuf.at[k, y_dn]),
        "w_down": (lambda k: wbuf.at[k, y], lambda k: wbuf.at[k, y], d_yd, lambda k: wbuf.at[k, y_up]),
        "w_up2": (lambda k: wbuf.at[k, y_dn, top], lambda k: wbuf.at[k, y_dn, top],
                  d_yu, lambda k: wbuf.at[k, y_far, top]),
        "w_down2": (lambda k: wbuf.at[k, y_up, bottom], lambda k: wbuf.at[k, y_up, bottom],
                    d_yd, lambda k: wbuf.at[k, y_far, bottom]),
        "hg_core": (lambda k: hg_in.at[:, cols(k, o)], lambda k: hgb.at[k, c],
                    d_c, lambda k: hgb.at[k, o]),
        "s1_up": (lambda k: part.at[k, x_far, 0], lambda k: r1.at[k, 0], d_xu, lambda k: r1.at[k, 0]),
        "s1_down": (lambda k: part.at[k, x_far, 1], lambda k: r1.at[k, 1], d_xd, lambda k: r1.at[k, 1]),
        "s2_up": (lambda k: part.at[k, x_up], lambda k: r2.at[k, 0], d_xu, lambda k: r2.at[k, 0]),
        "s2_down": (lambda k: part.at[k, x_dn], lambda k: r2.at[k, 1], d_xd, lambda k: r2.at[k, 1]),
        "z_pre": (lambda k: zs.at[k], lambda k: r3.at[k], d_z, lambda k: r3.at[k]),
        "z_grad": (lambda k: grad.at[k, x, h], lambda k: grad.at[k, x, h],
                   d_z, lambda k: grad.at[k, x, 1 - h]),
        "g_up": (lambda k: grad.at[k, x], lambda k: grad.at[k, x], d_xu, lambda k: grad.at[k, x_dn]),
        "g_down": (lambda k: grad.at[k, x], lambda k: grad.at[k, x], d_xd, lambda k: grad.at[k, x_up]),
        "g_up2": (lambda k: grad.at[k, x_dn, 0], lambda k: grad.at[k, x_dn, 0],
                  d_xu, lambda k: grad.at[k, x_far, 0]),
        "g_down2": (lambda k: grad.at[k, x_up, 1], lambda k: grad.at[k, x_up, 1],
                    d_xd, lambda k: grad.at[k, x_far, 1]),
        "hid_core": (lambda k: hs.at[k, o], lambda k: hid_out.at[:, cols(k, c)],
                     d_c, lambda k: hid_out.at[:, cols(k, o)]),
        "q1_up": (lambda k: q.at[k, y_far, top], lambda k: r8.at[k, 0], d_yu, lambda k: r8.at[k, 0]),
        "q1_down": (lambda k: q.at[k, y_far, bottom], lambda k: r8.at[k, 1], d_yd, lambda k: r8.at[k, 1]),
        "q2_up": (lambda k: q.at[k, y_up], lambda k: r9.at[k, 0], d_yu, lambda k: r9.at[k, 0]),
        "q2_down": (lambda k: q.at[k, y_dn], lambda k: r9.at[k, 1], d_yd, lambda k: r9.at[k, 1]),
        "wg_core": (lambda k: ws.at[k, o], lambda k: wg_out.at[:, cols(k, c)],
                    d_c, lambda k: wg_out.at[:, cols(k, o)]),
    }

    def desc(name, k):
        src, dst, to, _ = table[name]
        i = FLOWS.index(name)
        return rc(src(k), dst(k), f_send.at[i], f_recv.at[i, k], to)

    def start(name, k):
        @pl.when(k > 0)
        def _():
            desc(name, k - 1).wait_send()

        desc(name, k).start()

    def arrived(name, k):
        src, _, to, got = table[name]
        i = FLOWS.index(name)
        rc(src(k), got(k), f_send.at[i], f_recv.at[i, k], to).wait_recv()

    barrier = pltpu.get_barrier_semaphore()
    friends = (d_xu, d_xd, d_yu, d_yd, d_c, d_z, d_zu, d_zd)
    for d in friends:
        pl.semaphore_signal(barrier, inc=1, device_id=d, device_id_type=MESH)

    def w_local(k):
        return pltpu.make_async_copy(w_in.at[:, cols(k, c)], wbuf.at[k, y, w_rows(c)], w_loc.at[k])

    def hg_local(k):
        return pltpu.make_async_copy(hg_in.at[:, cols(k, c)], hgb.at[k, c], hg_loc.at[k])

    def hid_local(k):
        return pltpu.make_async_copy(hs.at[k, c], hid_out.at[:, cols(k, c)], hid_loc.at[k])

    def wg_local(k):
        return pltpu.make_async_copy(ws.at[k, c], wg_out.at[:, cols(k, c)], wg_loc.at[k])

    def spot(ref, b, g):
        return ref.at[pl.ds(2 * (b % 2), 2), b // 2, g]

    own_tok = pltpu.make_async_copy(tok_in, spot(tok, l, c), one_loc.at[0])
    own_tok.start()

    @pl.loop(0, NC)
    def _(k):
        w_local(k).start()

    pl.semaphore_wait(barrier, len(friends))

    def tok_z(b, way, step):
        return rc(spot(tok, b, c), spot(tok, b, c), t_send.at[way, step], t_recv.at[b],
                  d_zu if way == 0 else d_zd)

    def tok_c(b, g):
        return rc(spot(tok, b, g), spot(tok, b, g), tc_send.at[b], tc_recv.at[b], d_c)

    own_tok.wait()

    def tok_step(step):
        @pl.when((l < NL - 1) & (l >= step))
        def _():
            tok_z(l - step, 0, step).start()

        @pl.when((l > 0) & (l + step < NL))
        def _():
            tok_z(l + step, 1, step).start()

    def tok_take(step):
        @pl.when(l >= step)
        def _():
            tok_z(l - step, 0, step).wait_recv()

        @pl.when(l + step < NL)
        def _():
            tok_z(l + step, 1, step).wait_recv()

    def tok_hand(step):
        @pl.when(l >= step)
        def _():
            tok_c(l - step, c).start()

        @pl.when(l + step < NL)
        def _():
            tok_c(l + step, c).start()

    def w_a(k):
        w_local(k).wait()
        arrived("w_core", k)
        start("w_up", k)
        start("w_down", k)

    def w_b(k):
        arrived("w_up", k)
        start("w_up2", k)
        arrived("w_down", k)
        start("w_down2", k)

    tok_step(0)
    start("w_core", 0)
    start("w_core", 1)
    start("w_core", 2)
    tok_c(l, c).start()
    w_a(0)
    w_a(1)

    @pl.loop(3, NC)
    def _(k):
        start("w_core", k)

    tok_take(1)
    tok_step(1)
    tok_hand(1)
    w_b(0)
    w_a(2)
    tok_take(2)
    tok_step(2)
    tok_hand(2)
    tok_take(3)
    tok_hand(3)
    for b in range(NL):
        tok_c(b, o).wait_recv()
    acc[...] = jnp.zeros_like(acc)

    def pre_stage(k):
        arrived("w_up2", k)
        arrived("w_down2", k)
        hg_local(k).start()
        start("hg_core", k)

        def block(j):
            rows = tok[j].reshape(4 * SUB, D)
            out = jnp.dot(rows, wbuf[k].reshape(D, C), preferred_element_type=F32)
            part[k, j] = out.astype(BF).reshape(2, 2 * SUB, C)

        block(x_far)
        start("s1_up", k)
        start("s1_down", k)

        @pl.loop(0, 3)
        def _(s):
            block((x + 3 + s) % NX)

    def s2_stage(k):
        arrived("s1_up", k)
        part[k, x_up, 0] = (part[k, x_up, 0].astype(F32) + r1[k, 0].astype(F32)).astype(BF)
        start("s2_up", k)
        arrived("s1_down", k)
        part[k, x_dn, 1] = (part[k, x_dn, 1].astype(F32) + r1[k, 1].astype(F32)).astype(BF)
        start("s2_down", k)

    def s3_stage(k):
        arrived("s2_up", k)
        arrived("s2_down", k)

        def total(hh):
            return part[k, x, hh].astype(F32) + r2[k, 0, hh].astype(F32) + r2[k, 1, hh].astype(F32)

        zs[k] = total(1 - h).astype(BF)
        start("z_pre", k)
        tot[k] = total(h)

    def s4_stage(k):
        arrived("z_pre", k)
        hg_local(k).wait()
        arrived("hg_core", k)
        v = tot[k] + r3[k].astype(F32)
        hidden, slope = act_and_slope(v)
        gp = hgb[k].reshape(2 * SUB, C).astype(F32) * slope
        grad[k, x, h] = gp.astype(BF)
        start("z_grad", k)
        hs[k] = hidden.astype(BF).reshape(2, SUB, C)
        hid_local(k).start()
        start("hid_core", k)

    def s5_stage(k):
        arrived("z_grad", k)
        start("g_up", k)
        start("g_down", k)

    def s6_stage(k):
        arrived("g_up", k)
        start("g_up2", k)
        arrived("g_down", k)
        start("g_down2", k)

    def mm_stage(k):
        arrived("g_up2", k)
        arrived("g_down2", k)

        def wblock(j):
            rows = tok_t[pl.ds(pl.multiple_of(j * 2 * ROWS, 64), 2 * ROWS), :]
            out = jnp.dot(rows, grad[k].reshape(16 * SUB, C), preferred_element_type=F32)
            q[k, j] = out.astype(BF)

        wblock(y_far)
        start("q1_up", k)
        start("q1_down", k)

        @pl.loop(0, 3)
        def _(s):
            wblock((y + 3 + s) % NY)

        @pl.loop(0, NX)
        def _(j):
            out = lax.dot_general(
                grad[k, j].reshape(4 * SUB, C), wbuf[k].reshape(D, C), (((1,), (1,)), ((), ())),
                preferred_element_type=F32,
            )
            acc[j] += out

    def q2_stage(k):
        arrived("q1_up", k)
        q[k, y_up, top] = (q[k, y_up, top].astype(F32) + r8[k, 0].astype(F32)).astype(BF)
        start("q2_up", k)
        arrived("q1_down", k)
        q[k, y_dn, bottom] = (q[k, y_dn, bottom].astype(F32) + r8[k, 1].astype(F32)).astype(BF)
        start("q2_down", k)

    def q3_stage(k):
        arrived("q2_up", k)
        arrived("q2_down", k)
        t = q[k, y].astype(F32) + r9[k, 0].astype(F32) + r9[k, 1].astype(F32)
        ws[k] = (t * (1.0 / 64.0)).reshape(2, ROWS, C)
        wg_local(k).start()
        start("wg_core", k)

    def transpose_tokens():
        for j in range(NX):
            tok_t[:, j * 4 * SUB:(j + 1) * 4 * SUB] = tok[j].reshape(4 * SUB, D).T

    def stage(i, off, body):
        k = i - off

        @pl.when((k >= 0) & (k < NC))
        def _():
            body(k)

    @pl.loop(0, NC + 8)
    def _(i):
        stage(i, 4, s5_stage)
        stage(i, 5, s6_stage)
        stage(i, 1, s2_stage)
        stage(i, 0, pre_stage)
        stage(i, 2, s3_stage)
        stage(i, 3, s4_stage)
        stage(i, -1, w_b)
        stage(i, -3, w_a)
        stage(i, 6, mm_stage)
        stage(i, 7, q2_stage)
        stage(i, 8, q3_stage)
        pl.when(i == 1)(transpose_tokens)

    sums = acc.reshape(NX, 2, 2, SUB, D)
    for hh in range(2):
        cs[:, hh] = sums[:, hh, o].astype(BF)
    to_core = rc(cs, cr, c_sem.at[0], c_sem.at[1], d_c)
    to_core.start()
    to_core.wait_recv()

    def mine(b):
        s = pl.ds(2 * (b % 2), 2)
        return sums[s, b // 2, c] + cr[s, b // 2].astype(F32)

    def line(b, way):
        if way == 0:
            return rc(lr_send.at[b], lr_recv.at[b], lr_sems.at[0, b], lr_sems.at[1, b], d_zu)
        return rc(ll_send.at[b], ll_recv.at[b], ll_sems.at[0, b], ll_sems.at[1, b], d_zd)

    def go_right(b):
        @pl.when(l == 0)
        def _():
            lr_send[b] = mine(b).astype(BF)

        @pl.when((l > 0) & (l < b))
        def _():
            line(b, 0).wait_recv()
            lr_send[b] = (mine(b) + lr_recv[b].astype(F32)).astype(BF)

        @pl.when(l < b)
        def _():
            line(b, 0).start()

    def go_left(b):
        @pl.when(l == NL - 1)
        def _():
            ll_send[b] = mine(b).astype(BF)

        @pl.when((l < NL - 1) & (l > b))
        def _():
            line(b, 1).wait_recv()
            ll_send[b] = (mine(b) + ll_recv[b].astype(F32)).astype(BF)

        @pl.when(l > b)
        def _():
            line(b, 1).start()

    for b in range(NL - 1):
        go_right(NL - 1 - b)
        go_left(b)

    def finish(b):
        @pl.when(l == b)
        def _():
            t = mine(b)
            if b > 0:
                line(b, 0).wait_recv()
                t = t + lr_recv[b].astype(F32)
            if b < NL - 1:
                line(b, 1).wait_recv()
                t = t + ll_recv[b].astype(F32)
            ig_buf[...] = t.astype(BF)

    for b in range(NL):
        finish(b)
    out_ig = pltpu.make_async_copy(ig_buf, ig_out, one_loc.at[0])
    out_ig.start()

    last = NC - 1
    for name in FLOWS:
        desc(name, last).wait_send()

    @pl.loop(0, NC)
    def _(k):
        arrived("hid_core", k)
        arrived("wg_core", k)
        hid_local(k).wait()
        wg_local(k).wait()

    for step in range(NL - 1):
        @pl.when((l < NL - 1) & (l >= step))
        def _():
            tok_z(l - step, 0, step).wait_send()

        @pl.when((l > 0) & (l + step < NL))
        def _():
            tok_z(l + step, 1, step).wait_send()

    for b in range(NL):
        tok_c(b, c).wait_send()
    to_core.wait_send()
    for b in range(1, NL):
        @pl.when(l < b)
        def _():
            line(b, 0).wait_send()

    for b in range(NL - 1):
        @pl.when(l > b)
        def _():
            line(b, 1).wait_send()

    out_ig.wait()


def on_device(tokens, up_weight, hidden_grad):
    hbm = pl.BlockSpec(memory_space=pl.ANY)
    nf = len(FLOWS)
    dma = pltpu.SemaphoreType.DMA
    hidden, ig, wg = pl.pallas_call(
        kernel,
        out_shape=(
            jax.ShapeDtypeStruct((SUB, 2 * HALF), BF),
            jax.ShapeDtypeStruct((2, SUB, D), BF),
            jax.ShapeDtypeStruct((ROWS, 2 * HALF), F32),
        ),
        in_specs=[hbm] * 3,
        out_specs=[hbm] * 3,
        scratch_shapes=[
            pltpu.VMEM((NX, 2, 2, SUB, D), BF),
            pltpu.VMEM((D, 16 * SUB), BF),
            pltpu.VMEM((NC, NY, 2 * ROWS, C), BF),
            pltpu.VMEM((NC, 2, SUB, C), BF),
            pltpu.VMEM((NC, NX, 2, 2 * SUB, C), BF),
            pltpu.VMEM((NC, 2, 2 * SUB, C), BF),
            pltpu.VMEM((NC, 2, 2, 2 * SUB, C), BF),
            pltpu.VMEM((NC, 2 * SUB, C), BF),
            pltpu.VMEM((NC, 2 * SUB, C), BF),
            pltpu.VMEM((NC, 2 * SUB, C), F32),
            pltpu.VMEM((NC, NX, 2, 2 * SUB, C), BF),
            pltpu.VMEM((NC, 2, SUB, C), BF),
            pltpu.VMEM((NC, NY, 2 * ROWS, C), BF),
            pltpu.VMEM((NC, 2, ROWS, C), BF),
            pltpu.VMEM((NC, 2, 2 * ROWS, C), BF),
            pltpu.VMEM((NC, 2, ROWS, C), F32),
            pltpu.VMEM((NX, 4 * SUB, D), F32),
            pltpu.VMEM((NX, 2, SUB, D), BF),
            pltpu.VMEM((NX, 2, SUB, D), BF),
            pltpu.VMEM((NL, 2, SUB, D), BF),
            pltpu.VMEM((NL, 2, SUB, D), BF),
            pltpu.VMEM((NL, 2, SUB, D), BF),
            pltpu.VMEM((NL, 2, SUB, D), BF),
            pltpu.VMEM((2, SUB, D), BF),
            dma((nf,)), dma((nf, NC)),
            dma((NC,)), dma((NC,)), dma((NC,)), dma((NC,)), dma((1,)),
            dma((NL,)), dma((NL,)), dma((2, NL)), dma((NL,)), dma((2,)),
            dma((2, NL)), dma((2, NL)),
        ],
        name="block",
        compiler_params=pltpu.CompilerParams(
            collective_id=0, has_side_effects=True, vmem_limit_bytes=62 << 20
        ),
    )(tokens.reshape(2, SUB, D), up_weight, hidden_grad)
    return hidden, ig.reshape(2 * SUB, D), wg


def solution(mesh):
    placed = (P(("dep", "out"), "inp"), P(("inp", "dep"), "out"), P(("dep", "inp"), "out"))
    return jax.shard_map(
        on_device,
        mesh=mesh,
        in_specs=placed,
        out_specs=(P(("dep", "inp"), "out"), P(("dep", "out"), "inp"), P(("inp", "dep"), "out")),
        check_vma=False,
    )
```

time: 490 us -> 204 us (0.42)
  the two profiles are of different devices: /device:TPU:2 before, /device:TPU:1 now
where the time goes in v1:
time: 204 us; the launch traced here: 203 us
  Pallas kernels  196 us (96%)
  local copies, waits for them, and re-layouts  6.9 us (3%)
    pallas_call x1, Pallas kernels, on_device(): pl.pallas_call(kernel, out_shape=(jax.ShapeDtypeStruct((SUB, 2 * HALF), B...  196 us
    unnamed x3, local copies, waits for them, and re-layouts  6.9 us

profile of v1, /device:TPU:1, one launch (start us, length us, event | category | flops | bytes accessed | tf_op | source)
XLA Modules:
  0.0 203.5 jit_solution(10385557163855442824)
XLA Ops:
  0.6 196.0 %block.1 = (bf16[64,6144]{1,0:T(8,128)(2,1)}, bf16[2,64,768]{2,1,0:T(8,128)(2,1)}, f32[96,6144]{1,0:T(8,128)}) custom-call(bf16[2,64,768]{2,1,0:T(8,128)(2,1)} %bitcast.2, bf16[96,6144]{1,0:T(8,128)(2,1)} %w_in.1, bf16[64,6144]{1,0:T(8,128)(2,1)} %hg_in.1), custom_call_target="tpu_custom_call" | custom-call | tf_op jit(solution)/shard_map/block/pallas_call | solution.py:460
  196.6 2.1 %copy.9 = bf16[64,6144]{1,0:T(8,128)(2,1)} copy(bf16[64,6144]{1,0:T(8,128)(2,1)} %get-tuple-element.12) | data formatting | bytes 1572864
  198.7 1.6 copy.10
  200.3 3.2 %copy.11 = f32[96,6144]{1,0:T(8,128)} copy(f32[96,6144]{1,0:T(8,128)} %get-tuple-element.14) | data formatting | bytes 4718592

commit v2 on v1

v2 whole, which is shorter than its diff:
```python
import functools
import math

import jax
import jax.numpy as jnp
from jax import lax
from jax.experimental import pallas as pl
from jax.experimental.pallas import tpu as pltpu
from jax.sharding import PartitionSpec as P

MESH = pl.DeviceIdType.MESH
BF, F32 = jnp.bfloat16, jnp.float32

NX, NY, NL = 4, 4, 4
C, NC = 256, 12
HALF = C * NC
SUB = 64
ROWS = 96
D = 768
TOKENS = 4096
PARTS = 6

FLOWS = (
    "w_core", "w_up", "w_down", "w_up2", "w_down2", "hg_core",
    "s1_up", "s1_down", "s2_up", "s2_down", "z_pre", "z_grad",
    "g_up", "g_down", "g_up2", "g_down2", "hid_core",
    "q1_up", "q1_down", "q2_up", "q2_down", "wg_core",
)
SLOTS = 4
ORDER = (
    ("s6", 10), ("s5", 8), ("pre2", 2), ("pre1", 0), ("pre3", 4), ("s4", 6),
    ("w_b", -2), ("w_a", -3), ("s7", 12), ("q2", 14), ("q3", 16),
)


def act_and_slope(v):
    a, b = math.sqrt(2.0 / math.pi), 0.044715
    sq = v * v
    t = jnp.tanh(a * v * (1.0 + b * sq))
    half = 0.5 * (1.0 + t)
    return v * half, half + (0.5 * a) * v * (1.0 - t * t) * (1.0 + (3.0 * b) * sq)


def kernel(
    tok_in, w_in, hg_in, hid_out, ig_out, wg_out,
    tok, wbuf, hgb, s1, r1, s2, r2, zs, r3, tot, grad, hs, q, r8, r9, ws, acc, cs, cr,
    lr_send, lr_recv, ll_send, ll_recv, ig_buf, ig_bf,
    f_send, f_recv, w_loc, hg_loc, hid_loc, wg_loc, one_loc,
    t_recv, t_send, tc_recv, tc_send, c_send, c_recv, lr_ss, lr_rs, ll_ss, ll_rs,
):
    inp, l, dep = lax.axis_index("inp"), lax.axis_index("out"), lax.axis_index("dep")
    h, x = inp // NX, inp % NX
    y, c = dep // 2, dep % 2
    o = 1 - c

    def dev(h_=h, x_=x, l_=l, y_=y, c_=c):
        return (h_ * NX + x_, l_, y_ * 2 + c_)

    x_up, x_dn, x_far = (x + 1) % NX, (x + 3) % NX, (x + 2) % NX
    y_up, y_dn, y_far = (y + 1) % NY, (y + 3) % NY, (y + 2) % NY
    d_xu, d_xd, d_yu, d_yd = dev(x_=x_up), dev(x_=x_dn), dev(y_=y_up), dev(y_=y_dn)
    d_c, d_z = dev(c_=o), dev(h_=1 - h)
    zpos = h * NL + l
    zu, zd = (zpos + 1) % (2 * NL), (zpos + 2 * NL - 1) % (2 * NL)
    d_zu, d_zd = dev(h_=zu // NL, l_=zu % NL), dev(h_=zd // NL, l_=zd % NL)

    def rc(src, dst, ss, rs, to):
        return pltpu.make_async_remote_copy(
            src_ref=src, dst_ref=dst, send_sem=ss, recv_sem=rs, device_id=to, device_id_type=MESH
        )

    def cols(k, which):
        return pl.ds(pl.multiple_of(which * HALF + k * C, C), C)

    def w_rows(who):
        return pl.ds(pl.multiple_of(who * ROWS, 16), ROWS)

    top, bottom = pl.ds(0, ROWS), pl.ds(ROWS, ROWS)
    table = {
        "w_core": (lambda k: w_in.at[:, cols(k, o)], lambda k: wbuf.at[k, y, w_rows(c)],
                   d_c, lambda k: wbuf.at[k, y, w_rows(o)]),
        "w_up": (lambda k: wbuf.at[k, y], lambda k: wbuf.at[k, y], d_yu, lambda k: wbuf.at[k, y_dn]),
        "w_down": (lambda k: wbuf.at[k, y], lambda k: wbuf.at[k, y], d_yd, lambda k: wbuf.at[k, y_up]),
        "w_up2": (lambda k: wbuf.at[k, y_dn, top], lambda k: wbuf.at[k, y_dn, top],
                  d_yu, lambda k: wbuf.at[k, y_far, top]),
        "w_down2": (lambda k: wbuf.at[k, y_up, bottom], lambda k: wbuf.at[k, y_up, bottom],
                    d_yd, lambda k: wbuf.at[k, y_far, bottom]),
        "hg_core": (lambda k: hg_in.at[:, cols(k, o)], lambda k: hgb.at[k, c],
                    d_c, lambda k: hgb.at[k, o]),
        "s1_up": (lambda k: s1.at[k, 0], lambda k: r1.at[k, 0], d_xu, lambda k: r1.at[k, 0]),
        "s1_down": (lambda k: s1.at[k, 1], lambda k: r1.at[k, 1], d_xd, lambda k: r1.at[k, 1]),
        "s2_up": (lambda k: s2.at[k, 0], lambda k: r2.at[k, 0], d_xu, lambda k: r2.at[k, 0]),
        "s2_down": (lambda k: s2.at[k, 1], lambda k: r2.at[k, 1], d_xd, lambda k: r2.at[k, 1]),
        "z_pre": (lambda k: zs.at[k], lambda k: r3.at[k], d_z, lambda k: r3.at[k]),
        "z_grad": (lambda k: grad.at[k, x, h], lambda k: grad.at[k, x, h],
                   d_z, lambda k: grad.at[k, x, 1 - h]),
        "g_up": (lambda k: grad.at[k, x], lambda k: grad.at[k, x], d_xu, lambda k: grad.at[k, x_dn]),
        "g_down": (lambda k: grad.at[k, x], lambda k: grad.at[k, x], d_xd, lambda k: grad.at[k, x_up]),
        "g_up2": (lambda k: grad.at[k, x_dn, 0], lambda k: grad.at[k, x_dn, 0],
                  d_xu, lambda k: grad.at[k, x_far, 0]),
        "g_down2": (lambda k: grad.at[k, x_up, 1], lambda k: grad.at[k, x_up, 1],
                    d_xd, lambda k: grad.at[k, x_far, 1]),
        "hid_core": (lambda k: hs.at[k, o], lambda k: hid_out.at[:, cols(k, c)],
                     d_c, lambda k: hid_out.at[:, cols(k, o)]),
        "q1_up": (lambda k: q.at[k, y_far, top], lambda k: r8.at[k, 0], d_yu, lambda k: r8.at[k, 0]),
        "q1_down": (lambda k: q.at[k, y_far, bottom], lambda k: r8.at[k, 1], d_yd, lambda k: r8.at[k, 1]),
        "q2_up": (lambda k: q.at[k, y_up], lambda k: r9.at[k, 0], d_yu, lambda k: r9.at[k, 0]),
        "q2_down": (lambda k: q.at[k, y_dn], lambda k: r9.at[k, 1], d_yd, lambda k: r9.at[k, 1]),
        "wg_core": (lambda k: ws.at[k, o], lambda k: wg_out.at[:, cols(k, c)],
                    d_c, lambda k: wg_out.at[:, cols(k, o)]),
    }

    def desc(name, k):
        src, dst, to, _ = table[name]
        i = FLOWS.index(name)
        return rc(src(k), dst(k), f_send.at[i, k % SLOTS], f_recv.at[i, k], to)

    def when(cond, body):
        if isinstance(cond, bool):
            if cond:
                body()
        else:
            pl.when(cond)(body)

    def start(name, k):
        when(k >= SLOTS, lambda: desc(name, k - SLOTS).wait_send())
        desc(name, k).start()

    def arrived(name, k):
        src, _, to, got = table[name]
        i = FLOWS.index(name)
        rc(src(k), got(k), f_send.at[i, k % SLOTS], f_recv.at[i, k], to).wait_recv()

    barrier = pltpu.get_barrier_semaphore()
    friends = (d_xu, d_xd, d_yu, d_yd, d_c, d_z, d_zu, d_zd)
    for d in friends:
        pl.semaphore_signal(barrier, inc=1, device_id=d, device_id_type=MESH)

    def w_local(k):
        return pltpu.make_async_copy(w_in.at[:, cols(k, c)], wbuf.at[k, y, w_rows(c)], w_loc.at[k])

    def hg_local(k):
        return pltpu.make_async_copy(hg_in.at[:, cols(k, c)], hgb.at[k, c], hg_loc.at[k])

    def hid_local(k):
        return pltpu.make_async_copy(hs.at[k, c], hid_out.at[:, cols(k, c)], hid_loc.at[k])

    def wg_local(k):
        return pltpu.make_async_copy(ws.at[k, c], wg_out.at[:, cols(k, c)], wg_loc.at[k])

    def spot(ref, b, g):
        return ref.at[pl.ds(2 * (b % 2), 2), b // 2, g]

    own_tok = pltpu.make_async_copy(tok_in, spot(tok, l, c), one_loc.at[0])
    own_tok.start()

    @pl.loop(0, NC)
    def _(k):
        w_local(k).start()

    pl.semaphore_wait(barrier, len(friends))

    def tok_z(j, hh, way):
        return rc(tok.at[j, hh, c], tok.at[j, hh, c], t_send.at[way, j, hh], t_recv.at[j, hh],
                  d_zu if way == 0 else d_zd)

    def tok_c(j, hh, g):
        return rc(tok.at[j, hh, g], tok.at[j, hh, g], tc_send.at[j, hh], tc_recv.at[j, hh], d_c)

    def tok_step(j, step):
        for hh in range(2):
            b = j // 2 + 2 * hh

            def right():
                tok_z(j, hh, 0).start()

            def left():
                tok_z(j, hh, 1).start()

            def pass_on(ways):
                if step > 0:
                    tok_z(j, hh, 0).wait_recv()
                for cond, send in ways:
                    pl.when(cond)(send)
                tok_c(j, hh, c).start()

            if step == 0:
                pl.when(l == b)(lambda: pass_on(((l < NL - 1, right), (l > 0, left))))
            else:
                pl.when(l == b + step)(lambda: pass_on(((l < NL - 1, right),)))
                pl.when(l == b - step)(lambda: pass_on(((l > 0, left),)))

    def tok_ready(j):
        for hh in range(2):
            tok_c(j, hh, 1 - c).wait_recv()

    def dot_pre(j, k):
        rows = tok[j].reshape(4 * SUB, D)
        return jnp.dot(rows, wbuf[k].reshape(D, C), preferred_element_type=F32)

    def add_input(j, k):
        acc[j] += lax.dot_general(
            grad[k, j].reshape(4 * SUB, C), wbuf[k].reshape(D, C), (((1,), (1,)), ((), ())),
            preferred_element_type=F32,
        )

    def w_a(k):
        w_local(k).wait()
        arrived("w_core", k)
        start("w_up", k)
        start("w_down", k)

    def w_b(k):
        arrived("w_up", k)
        start("w_up2", k)
        arrived("w_down", k)
        start("w_down2", k)

    def pre1(k):
        arrived("w_up2", k)
        arrived("w_down2", k)
        s1[k] = dot_pre(x_far, k).astype(BF).reshape(2, 2 * SUB, C)
        start("s1_up", k)
        start("s1_down", k)
        hg_local(k).start()
        start("hg_core", k)

    def pre2(k):
        out = dot_pre(x_up, k).reshape(2, 2 * SUB, C)
        arrived("s1_up", k)
        s2[k, 0, 0] = (out[0] + r1[k, 0].astype(F32)).astype(BF)
        s2[k, 0, 1] = out[1].astype(BF)
        start("s2_up", k)
        out = dot_pre(x_dn, k).reshape(2, 2 * SUB, C)
        arrived("s1_down", k)
        s2[k, 1, 0] = out[0].astype(BF)
        s2[k, 1, 1] = (out[1] + r1[k, 1].astype(F32)).astype(BF)
        start("s2_down", k)

    def pre3(k):
        out = dot_pre(x, k).reshape(2, 2 * SUB, C)
        arrived("s2_up", k)
        arrived("s2_down", k)
        tot[k] = out + r2[k, 0].astype(F32) + r2[k, 1].astype(F32)
        zs[k] = tot[k, 1 - h].astype(BF)
        start("z_pre", k)

    def s4(k):
        hg_local(k).wait()
        arrived("hg_core", k)
        arrived("z_pre", k)
        v = tot[k, h] + r3[k].astype(F32)
        hidden, slope = act_and_slope(v)
        gp = hgb[k].reshape(2 * SUB, C).astype(F32) * slope
        grad[k, x, h] = gp.astype(BF)
        start("z_grad", k)
        hs[k] = hidden.astype(BF).reshape(2, SUB, C)
        hid_local(k).start()
        start("hid_core", k)

    def s5(k):
        arrived("z_grad", k)
        start("g_up", k)
        start("g_down", k)
        add_input(x, k)

    def s6(k):
        arrived("g_up", k)
        start("g_up2", k)
        arrived("g_down", k)
        start("g_down2", k)
        add_input(x_up, k)
        add_input(x_dn, k)

    def s7(k):
        arrived("g_up2", k)
        arrived("g_down2", k)
        add_input(x_far, k)
        out = lax.dot_general(
            tok[...].reshape(16 * SUB, D), grad[k].reshape(16 * SUB, C), (((0,), (0,)), ((), ())),
            preferred_element_type=F32,
        )
        q[k] = out.astype(BF).reshape(NY, 2 * ROWS, C)
        start("q1_up", k)
        start("q1_down", k)

    def q2(k):
        arrived("q1_up", k)
        q[k, y_up, top] = (q[k, y_up, top].astype(F32) + r8[k, 0].astype(F32)).astype(BF)
        start("q2_up", k)
        arrived("q1_down", k)
        q[k, y_dn, bottom] = (q[k, y_dn, bottom].astype(F32) + r8[k, 1].astype(F32)).astype(BF)
        start("q2_down", k)

    def q3(k):
        arrived("q2_up", k)
        arrived("q2_down", k)
        t = q[k, y].astype(F32) + r9[k, 0].astype(F32) + r9[k, 1].astype(F32)
        ws[k] = t.astype(BF).reshape(2, ROWS, C)
        wg_local(k).start()
        start("wg_core", k)

    stages = dict(w_a=w_a, w_b=w_b, pre1=pre1, pre2=pre2, pre3=pre3, s4=s4, s5=s5, s6=s6, s7=s7,
                  q2=q2, q3=q3)
    offset = dict(ORDER)

    def run(i, after=None):
        for name, off in ORDER:
            k = i - off
            body = stages[name]
            if isinstance(k, int):
                if 0 <= k < NC:
                    body(k)
                    if after is not None and k == NC - 1 and name in after:
                        after[name]()
            else:
                pl.when((k >= 0) & (k < NC))(functools.partial(body, k))

    sums = acc.reshape(NX, 2, 2, SUB, D)

    def to_core(j):
        return rc(cs.at[j], cr.at[j], c_send.at[j], c_recv.at[j], d_c)

    def ig_give(j):
        for hh in range(2):
            cs[j, hh] = sums[j, hh, o].astype(BF)
        to_core(j).start()

    def mine(j, hh):
        return sums[j, hh, c] + cr[j, hh].astype(F32)

    def line(j, hh, way):
        if way == 0:
            return rc(lr_send.at[j, hh], lr_recv.at[j, hh], lr_ss.at[j, hh], lr_rs.at[j, hh], d_zu)
        return rc(ll_send.at[j, hh], ll_recv.at[j, hh], ll_ss.at[j, hh], ll_rs.at[j, hh], d_zd)

    def ig_step(j, step):
        if step == 0:
            to_core(j).wait_recv()
        for hh in range(2):
            b = j // 2 + 2 * hh

            def move(way):
                out_buf, in_buf = (lr_send, lr_recv) if way == 0 else (ll_send, ll_recv)
                t = mine(j, hh)
                if step > 0:
                    line(j, hh, way).wait_recv()
                    t = t + in_buf[j, hh].astype(F32)
                out_buf[j, hh] = t.astype(BF)
                line(j, hh, way).start()

            pl.when((l == step) & (b > l))(functools.partial(move, 0))
            pl.when((l == NL - 1 - step) & (b < l))(functools.partial(move, 1))

    def ig_end(j):
        for hh in range(2):
            b = j // 2 + 2 * hh

            @pl.when(l == b)
            def _():
                spot_ = j % 2
                ig_buf[spot_] = mine(j, hh)

                @pl.when(l > 0)
                def _():
                    line(j, hh, 0).wait_recv()
                    ig_buf[spot_] += lr_recv[j, hh].astype(F32)

                @pl.when(l < NL - 1)
                def _():
                    line(j, hh, 1).wait_recv()
                    ig_buf[spot_] += ll_recv[j, hh].astype(F32)

                ig_bf[spot_] = ig_buf[spot_].astype(BF)

    own_tok.wait()
    start("w_core", 0)
    tok_step(x_far, 0)
    w_a(0)
    for k in range(1, SLOTS):
        start("w_core", k)
    tok_step(x_up, 0)
    w_a(1)
    tok_step(x_far, 1)
    tok_step(x_dn, 0)
    w_b(0)
    tok_step(x_up, 1)
    tok_step(x_far, 2)
    tok_step(x, 0)

    @pl.loop(SLOTS, NC)
    def _(k):
        start("w_core", k)

    acc[...] = jnp.zeros_like(acc)
    tok_step(x_dn, 1)
    tok_step(x_up, 2)
    w_b(1)
    w_a(2)
    tok_step(x_far, 3)
    tok_ready(x_far)
    run(0)
    tok_step(x, 1)
    tok_step(x_dn, 2)
    tok_step(x_up, 3)
    run(1)
    tok_step(x, 2)
    tok_step(x_dn, 3)
    tok_step(x, 3)
    tok_ready(x_up)
    tok_ready(x_dn)
    tok_ready(x)

    first_end = offset["s5"] + NC - 1
    pl.loop(2, first_end)(run)

    def after_s6():
        ig_step(x, 0)
        ig_give(x_up)
        ig_give(x_dn)
        ig_step(x, 1)

    def after_s7():
        ig_give(x_far)
        ig_step(x_up, 0)
        ig_step(x_dn, 0)
        ig_step(x, 2)
        ig_step(x_far, 0)
        ig_step(x_up, 1)
        ig_step(x_dn, 1)

    def after_q2():
        ig_step(x_far, 1)
        ig_step(x_up, 2)
        ig_step(x_dn, 2)
        ig_step(x_far, 2)

    after = {"s5": lambda: ig_give(x), "s6": after_s6, "s7": after_s7, "q2": after_q2}
    for i in range(first_end, offset["q3"] + NC):
        run(i, after)
    for j in (x, x_up, x_dn, x_far):
        ig_end(j)
    out_ig = pltpu.make_async_copy(ig_bf, ig_out, one_loc.at[0])
    out_ig.start()

    for name in FLOWS:
        for k in range(NC - SLOTS, NC):
            desc(name, k).wait_send()

    @pl.loop(0, NC)
    def _(k):
        arrived("hid_core", k)
        arrived("wg_core", k)
        hid_local(k).wait()
        wg_local(k).wait()

    for j in range(NX):
        for hh in range(2):
            b = j // 2 + 2 * hh
            pl.when((l >= b) & (l < NL - 1))(lambda: tok_z(j, hh, 0).wait_send())
            pl.when((l <= b) & (l > 0))(lambda: tok_z(j, hh, 1).wait_send())
            tok_c(j, hh, c).wait_send()
            pl.when(l < b)(lambda: line(j, hh, 0).wait_send())
            pl.when(l > b)(lambda: line(j, hh, 1).wait_send())
        to_core(j).wait_send()
    out_ig.wait()


def finish_kernel(hid_in, ig_in, wg_in, hid_out, ig_out, wg_out, hid, ig, half, full, in_sems, out_sems):
    rows = ROWS // PARTS

    def load(p):
        return pltpu.make_async_copy(wg_in.at[pl.ds(p * rows, rows)], half.at[p], in_sems.at[p])

    def store(p):
        return pltpu.make_async_copy(full.at[p], wg_out.at[pl.ds(p * rows, rows)], out_sems.at[p])

    through = (
        (pltpu.make_async_copy(hid_in, hid, in_sems.at[PARTS]),
         pltpu.make_async_copy(hid, hid_out, out_sems.at[PARTS])),
        (pltpu.make_async_copy(ig_in, ig, in_sems.at[PARTS + 1]),
         pltpu.make_async_copy(ig, ig_out, out_sems.at[PARTS + 1])),
    )
    for p in range(PARTS):
        load(p).start()
    for come, _ in through:
        come.start()
    for p in range(PARTS):
        load(p).wait()
        full[p] = half[p].astype(F32) * (1.0 / math.sqrt(TOKENS))
        store(p).start()
    for come, go in through:
        come.wait()
        go.start()
    for p in range(PARTS):
        store(p).wait()
    for _, go in through:
        go.wait()


def on_device(tokens, up_weight, hidden_grad):
    hbm = pl.BlockSpec(memory_space=pl.ANY)
    nf = len(FLOWS)
    dma = pltpu.SemaphoreType.DMA
    hidden, ig, wg = pl.pallas_call(
        kernel,
        out_shape=(
            jax.ShapeDtypeStruct((SUB, 2 * HALF), BF),
            jax.ShapeDtypeStruct((2, SUB, D), BF),
            jax.ShapeDtypeStruct((ROWS, 2 * HALF), BF),
        ),
        in_specs=[hbm] * 3,
        out_specs=[hbm] * 3,
        scratch_shapes=[
            pltpu.VMEM((NX, 2, 2, SUB, D), BF),
            pltpu.VMEM((NC, NY, 2 * ROWS, C), BF),
            pltpu.VMEM((NC, 2, SUB, C), BF),
            pltpu.VMEM((NC, 2, 2 * SUB, C), BF),
            pltpu.VMEM((NC, 2, 2 * SUB, C), BF),
            pltpu.VMEM((NC, 2, 2, 2 * SUB, C), BF),
            pltpu.VMEM((NC, 2, 2, 2 * SUB, C), BF),
            pltpu.VMEM((NC, 2 * SUB, C), BF),
            pltpu.VMEM((NC, 2 * SUB, C), BF),
            pltpu.VMEM((NC, 2, 2 * SUB, C), F32),
            pltpu.VMEM((NC, NX, 2, 2 * SUB, C), BF),
            pltpu.VMEM((NC, 2, SUB, C), BF),
            pltpu.VMEM((NC, NY, 2 * ROWS, C), BF),
            pltpu.VMEM((NC, 2, ROWS, C), BF),
            pltpu.VMEM((NC, 2, 2 * ROWS, C), BF),
            pltpu.VMEM((NC, 2, ROWS, C), BF),
            pltpu.VMEM((NX, 4 * SUB, D), F32),
            pltpu.VMEM((NX, 2, SUB, D), BF),
            pltpu.VMEM((NX, 2, SUB, D), BF),
            pltpu.VMEM((NX, 2, SUB, D), BF),
            pltpu.VMEM((NX, 2, SUB, D), BF),
            pltpu.VMEM((NX, 2, SUB, D), BF),
            pltpu.VMEM((NX, 2, SUB, D), BF),
            pltpu.VMEM((2, SUB, D), F32),
            pltpu.VMEM((2, SUB, D), BF),
            dma((nf, SLOTS)), dma((nf, NC)),
            dma((NC,)), dma((NC,)), dma((NC,)), dma((NC,)), dma((1,)),
            dma((NX, 2)), dma((2, NX, 2)), dma((NX, 2)), dma((NX, 2)), dma((NX,)), dma((NX,)),
            dma((NX, 2)), dma((NX, 2)), dma((NX, 2)), dma((NX, 2)),
        ],
        name="block",
        compiler_params=pltpu.CompilerParams(
            collective_id=0, has_side_effects=True, vmem_limit_bytes=62 << 20
        ),
    )(tokens.reshape(2, SUB, D), up_weight, hidden_grad)
    hidden, ig, wg = pl.pallas_call(
        finish_kernel,
        out_shape=(
            jax.ShapeDtypeStruct((SUB, 2 * HALF), BF),
            jax.ShapeDtypeStruct((2, SUB, D), BF),
            jax.ShapeDtypeStruct((ROWS, 2 * HALF), F32),
        ),
        in_specs=[hbm] * 3,
        out_specs=[hbm] * 3,
        scratch_shapes=[
            pltpu.VMEM((SUB, 2 * HALF), BF),
            pltpu.VMEM((2, SUB, D), BF),
            pltpu.VMEM((PARTS, ROWS // PARTS, 2 * HALF), BF),
            pltpu.VMEM((PARTS, ROWS // PARTS, 2 * HALF), F32),
            dma((PARTS + 2,)), dma((PARTS + 2,)),
        ],
        name="finish",
        compiler_params=pltpu.CompilerParams(vmem_limit_bytes=62 << 20),
    )(hidden, ig, wg)
    return hidden, ig.reshape(2 * SUB, D), wg


def solution(mesh):
    placed = (P(("dep", "out"), "inp"), P(("inp", "dep"), "out"), P(("dep", "inp"), "out"))
    return jax.shard_map(
        on_device,
        mesh=mesh,
        in_specs=placed,
        out_specs=(P(("dep", "inp"), "out"), P(("dep", "out"), "inp"), P(("inp", "dep"), "out")),
        check_vma=False,
    )
```

time: 204 us -> 164 us (0.80)
  the two profiles are of different devices: /device:TPU:1 before, /device:TPU:2 now
where the time goes in v2:
time: 164 us; the launch traced here: 163 us
  Pallas kernels  162 us (99%)
    pallas_call x1, Pallas kernels, on_device(): pl.pallas_call(kernel, out_shape=(jax.ShapeDtypeStruct((SUB, 2 * HALF), B...  160 us

profile of v2, /device:TPU:2, one launch (start us, length us, event | category | flops | bytes accessed | tf_op | source)
XLA Modules:
  0.0 163.0 jit_solution(12726815545764378287)
XLA Ops:
  0.6 159.5 %block.1 = (bf16[64,6144]{1,0:T(8,128)(2,1)}, bf16[2,64,768]{2,1,0:T(8,128)(2,1)}, bf16[96,6144]{1,0:T(8,128)(2,1)}) custom-call(bf16[2,64,768]{2,1,0:T(8,128)(2,1)} %bitcast.2, bf16[96,6144]{1,0:T(8,128)(2,1)} %w_in.1, bf16[64,6144]{1,0:T(8,128)(2,1)} %hg_in.1), custom_call_target="tpu_custom_call" | custom-call | tf_op jit(solution)/shard_map/block/pallas_call | solution.py:505
  160.2 2.8 %finish.1 = (bf16[64,6144]{1,0:T(8,128)(2,1)}, bf16[2,64,768]{2,1,0:T(8,128)(2,1)}, f32[96,6144]{1,0:T(8,128)}) custom-call(bf16[64,6144]{1,0:T(8,128)(2,1)} %get-tuple-element.9.hid_in, bf16[2,64,768]{2,1,0:T(8,128)(2,1)} %get-tuple-element.10.ig_in, bf16[96,6144]{1,0:T(8,128)(2,1)} %get-tuple-element.11.wg_in), custom_call_target="tpu_custom_call" | custom-call | tf_op jit(solution)/shard_map/finish/pallas_call | solution.py:550

commit v3 on v2

--- a/solution.py
+++ b/solution.py
@@ -28,8 +28,8 @@
 )
 SLOTS = 4
 ORDER = (
-    ("s6", 10), ("s5", 8), ("pre2", 2), ("pre1", 0), ("pre3", 4), ("s4", 6),
-    ("w_b", -2), ("w_a", -3), ("s7", 12), ("q2", 14), ("q3", 16),
+    ("s6", 12), ("s5", 10), ("pre2", 2), ("pre1", 0), ("pre3", 4), ("s4", 7),
+    ("w_b", -2), ("w_a", -3), ("s7", 14), ("q2", 16), ("q3", 18),
 )
 
 

time: 164 us -> 165 us (level)
  no operation moved by 1% of the time
where the time goes in v3:
time: 165 us; the launch traced here: 164 us
  Pallas kernels  163 us (99%)
    pallas_call x1, Pallas kernels, on_device(): pl.pallas_call(kernel, out_shape=(jax.ShapeDtypeStruct((SUB, 2 * HALF), B...  160 us

profile of v3, /device:TPU:2, one launch (start us, length us, event | category | flops | bytes accessed | tf_op | source)
XLA Modules:
  0.0 163.8 jit_solution(3839324468504836426)
XLA Ops:
  0.6 160.3 %block.1 = (bf16[64,6144]{1,0:T(8,128)(2,1)}, bf16[2,64,768]{2,1,0:T(8,128)(2,1)}, bf16[96,6144]{1,0:T(8,128)(2,1)}) custom-call(bf16[2,64,768]{2,1,0:T(8,128)(2,1)} %bitcast.2, bf16[96,6144]{1,0:T(8,128)(2,1)} %w_in.1, bf16[64,6144]{1,0:T(8,128)(2,1)} %hg_in.1), custom_call_target="tpu_custom_call" | custom-call | tf_op jit(solution)/shard_map/block/pallas_call | solution.py:505
  161.0 2.8 %finish.1 = (bf16[64,6144]{1,0:T(8,128)(2,1)}, bf16[2,64,768]{2,1,0:T(8,128)(2,1)}, f32[96,6144]{1,0:T(8,128)}) custom-call(bf16[64,6144]{1,0:T(8,128)(2,1)} %get-tuple-element.9.hid_in, bf16[2,64,768]{2,1,0:T(8,128)(2,1)} %get-tuple-element.10.ig_in, bf16[96,6144]{1,0:T(8,128)(2,1)} %get-tuple-element.11.wg_in), custom_call_target="tpu_custom_call" | custom-call | tf_op jit(solution)/shard_map/finish/pallas_call | solution.py:550
